TPU v7x, 256 devices: a whole 4x4x8 slice. The times are simulated.
256 devices in a mesh: dp: 256 (over y, z, x, core).
Axes of the slice: x: 4, y: 4, z: 8, core: 2. Of those that a mesh axis runs over, the one named last changes fastest.
Arguments:
- image_feat: bfloat16 [131072, 1152], P('dp'), may hold values from -6 to 6
- text_feat: bfloat16 [131072, 1152], P('dp'), may hold values from -6 to 6
- image_proj: bfloat16 [1152, 1152], replicated, may hold values from -0.1875 to 0.1875
- text_proj: bfloat16 [1152, 1152], replicated, may hold values from -0.1875 to 0.1875
- logit_scale_logarithm: float32 [1], replicated, may hold values from 0 to 1.5
- bias: float32 [1], replicated, may hold values from -2 to 0
- counts: int32 [256], P('dp'), may hold values from 1 to 4, 512 in all
Outputs:
- image_proj_grad: float32 [1327104], P('dp')
- text_proj_grad: float32 [1327104], P('dp')
Inputs may be any that keep to these rules, and one draw needn't show every extreme that they name: counts holds whole pair blocks of 128 pairs; the counts sum to 512, and at least one device holds 4 blocks.
All inputs are finite; a program needn't handle non-finite values.
Results may differ from a plain program's by a relative error of at most 0.0043.
Values may be sent and summed in bfloat16 or wider, within the bound.
No kernel may reach another device: no remote copies, remote signals or barrier semaphores. Data moves between devices by JAX's collectives and lax.ppermute only.
A program may use at most 128 MiB of HBM per device.

v0:
```python
import functools

import jax
import jax.numpy as jnp
import numpy as np
from jax import lax
from jax.experimental import pallas as pl
from jax.experimental.pallas import tpu as pltpu
from jax.sharding import PartitionSpec as P

BLK = 128
D = 1152
R = 512
NY, NZ, NX = 4, 8, 4
N = 256
OWN = 9
PART = 384
GRANTS = (10,10,12,10,10)
BF = jnp.bfloat16
F32 = jnp.float32
VMEM = pl.BlockSpec(memory_space=pltpu.VMEM)
SMEM = pl.BlockSpec(memory_space=pltpu.SMEM)


def dev(y, z, x, c):
    return ((y * NZ + z) * NX + x) * 2 + c


PLANES = [
    [dev(y, z, x, c) for y in range(NY) for x in range(NX)]
    for z in range(NZ)
    for c in range(2)
]
COLUMNS = [
    [dev(y, z, x, c) for z in range(NZ) for c in range(2)]
    for y in range(NY)
    for x in range(NX)
]
SWAP = [(d, d ^ 1) for d in range(N)]


def shuffle_matrix():
    i = lax.optimization_barrier(lax.iota(jnp.int32, D))
    group = i // OWN
    y, x, z = group // (NX * NZ), group // NZ % NX, group % NZ
    source = ((y * NZ + z) * NX + x) * OWN + i % OWN
    return (source[:, None] == lax.broadcasted_iota(jnp.int32, (D, D), 1)).astype(BF)


def shift(value, steps):
    return lax.ppermute(value, "dp", [(d, (d + steps) % N) for d in range(N)])


def mm(a, b):
    return jnp.dot(a, b, preferred_element_type=F32)


def mm_t(a, b):
    return lax.dot_general(a, b, (((1,), (1,)), ((), ())), preferred_element_type=F32)


def t_mm(a, b):
    return lax.dot_general(a, b, (((0,), (0,)), ((), ())), preferred_element_type=F32)


def project(feat_ref, proj_ref, dir_ref, unit_ref, inv_ref, base=0):
    for i in range(R // BLK):
        rows = slice(i * BLK, (i + 1) * BLK)
        raw = mm(feat_ref[rows, :], proj_ref[...])
        inverse = 1.0 / jnp.sqrt(jnp.sum(raw * raw, axis=1, keepdims=True) + 1e-06)
        direction = raw * inverse
        dir_ref[rows, :] = direction
        unit_ref[base + i * BLK:base + (i + 1) * BLK, :] = direction.astype(BF)
        inv_ref[rows, :] = inverse


def turned(feat_ref, shuffle_ref, out_ref):
    out_ref[...] = mm_t(shuffle_ref[...], feat_ref[...]).astype(BF)


def raw_grad(gradient, direction, inverse):
    radial = jnp.sum(direction * gradient, axis=1, keepdims=True)
    return ((gradient - direction * radial) * inverse).astype(BF)


def first_kernel(scal, text, image, text_proj, image_proj, shuffle,
                 dir_t, unit_t, inv_t, turn_t, dir_i, unit_i, inv_i, turn_i, grad_i, pair):
    scale, bias = scal[0], scal[1]
    project(text, text_proj, dir_t, unit_t, inv_t)
    project(image, image_proj, dir_i, unit_i, inv_i)
    logit = scale * mm_t(unit_i[...], unit_t[...]) + bias
    same = lax.broadcasted_iota(jnp.int32, (R, R), 0) == lax.broadcasted_iota(jnp.int32, (R, R), 1)
    sign = jnp.where(same, -1.0, 1.0)
    pair[...] = (sign * jax.nn.sigmoid(sign * logit)).astype(BF)
    grad_i[...] = mm(pair[...], unit_t[...])
    turned(text, shuffle, turn_t)
    turned(image, shuffle, turn_i)


def second_kernel(scal, image1, image_proj, shuffle, unit_i0, unit_t0, dir_t0, inv_t0, pair0,
                  dir_i1, unit_i, inv_i1, turn_i1, grad_i1, delta_t0, pair):
    scale, bias = scal[0], scal[1]
    unit_i[:R, :] = unit_i0[...]
    pair[:R, :] = pair0[...]
    project(image1, image_proj, dir_i1, unit_i, inv_i1, R)
    logit = scale * mm_t(unit_i[R:, :], unit_t0[...]) + bias
    pair[R:, :] = jax.nn.sigmoid(logit).astype(BF)
    grad_i1[...] = mm(pair[R:, :], unit_t0[...])
    delta_t0[...] = raw_grad(scale * t_mm(pair[...], unit_i[...]), dir_t0[...], inv_t0[...])
    turned(image1, shuffle, turn_i1)


def third_kernel(scal, text2, text_proj, shuffle, unit_i, dir_i0, dir_i1, inv_i0, inv_i1, grad_i0, grad_i1,
                 delta_i, delta_t2, turn_t2, dir_t2, unit_t2, inv_t2, pair):
    scale, bias = scal[0], scal[1]
    project(text2, text_proj, dir_t2, unit_t2, inv_t2)
    for dir_i, inv_i, grad_i, base in ((dir_i0, inv_i0, grad_i0, 0), (dir_i1, inv_i1, grad_i1, R)):
        rows = slice(base, base + R)
        logit = scale * mm_t(unit_i[rows, :], unit_t2[...]) + bias
        pair[rows, :] = jax.nn.sigmoid(logit).astype(BF)
        gradient = scale * (grad_i[...] + mm(pair[rows, :], unit_t2[...]))
        delta_i[rows, :] = raw_grad(gradient, dir_i[...], inv_i[...])
    delta_t2[...] = raw_grad(scale * t_mm(pair[...], unit_i[...]), dir_t2[...], inv_t2[...])
    turned(text2, shuffle, turn_t2)


def term_kernel(image_core, which, turn_i0, turn_i1, delta_i, turn_t0, turn_t2, delta_t0, delta_t2, out):
    def total(turn_a, turn_b, delta_a, delta_b):
        @pl.loop(0, D // PART)
        def _(i):
            rows = pl.ds(pl.multiple_of(i * PART, PART), PART)
            out[rows, :] = (
                mm(turn_a[rows, :], delta_a[...]) + mm(turn_b[rows, :], delta_b[...])
            ).astype(out.dtype)

    @pl.when(which[0] == image_core)
    def _():
        total(turn_i0, turn_i1, delta_i.at[:R], delta_i.at[R:])

    @pl.when(which[0] != image_core)
    def _():
        total(turn_t0, turn_t2, delta_t0, delta_t2)


def join_kernel(plane, out):
    total = jnp.sum(plane[...].astype(F32), axis=0)
    for z in range(NZ):
        for h in range(2):
            out[2 * z + h] = total[OWN * z + 4 * h:OWN * z + 4 * h + 5, :].astype(BF)


def call(kernel, operands, outs, scratch=(), flops=0, name=None, grant=8):
    shapes = [jax.ShapeDtypeStruct(shape, kind) for shape, kind in outs]
    moved = sum(a.size * a.dtype.itemsize for a in operands)
    moved += sum(int(np.prod(s.shape)) * s.dtype.itemsize for s in shapes)
    return pl.pallas_call(
        kernel,
        out_shape=shapes,
        in_specs=[SMEM if a.size < 8 else VMEM for a in operands],
        out_specs=[VMEM] * len(shapes),
        scratch_shapes=[pltpu.VMEM(shape, kind) for shape, kind in scratch],
        compiler_params=pltpu.CompilerParams(vmem_limit_bytes=grant << 20),
        cost_estimate=pl.CostEstimate(flops=flops, bytes_accessed=moved, transcendentals=0),
        name=name,
    )(*operands)


def local(image_feat, text_feat, image_proj, text_proj, logit_scale_logarithm, bias, counts):
    scal = jnp.stack([jnp.exp(logit_scale_logarithm[0]), bias[0]])
    rows = lax.broadcasted_iota(jnp.int32, image_feat.shape, 0)
    live = rows < counts[0] * BLK
    zero = jnp.zeros((), BF)
    text0 = jnp.where(live, text_feat, zero)
    image_feat, text0 = lax.optimization_barrier((image_feat, text0))
    image0 = jnp.where(live, image_feat, zero)
    text2 = shift(text0, 2)
    image1 = shift(image0, -1)
    shuffle = shuffle_matrix()
    me = lax.axis_index("dp")
    core = me % 2

    unit, wide, line, turn = ((R, D), BF), ((R, D), F32), ((R, 1), F32), ((D, R), BF)
    step = 2 * R * D * D
    dir_t0, unit_t0, inv_t0, turn_t0, dir_i0, unit_i0, inv_i0, turn_i0, grad_i0, pair0 = call(
        first_kernel,
        (scal, text0, image0, text_proj, image_proj, shuffle),
        [wide, unit, line, turn] * 2 + [wide, ((R, R), BF)],
        flops=5 * step,
        name="own_rows",
        grant=GRANTS[0],
    )
    dir_i1, unit_i, inv_i1, turn_i1, grad_i1, delta_t0 = call(
        second_kernel,
        (scal, image1, image_proj, shuffle, unit_i0, unit_t0, dir_t0, inv_t0, pair0),
        [wide, ((2 * R, D), BF), line, turn, wide, unit],
        [((2 * R, R), BF)],
        flops=4 * step,
        name="own_texts",
        grant=GRANTS[1],
    )
    delta_i, delta_t2, turn_t2 = call(
        third_kernel,
        (scal, text2, text_proj, shuffle, unit_i, dir_i0, dir_i1, inv_i0, inv_i1, grad_i0, grad_i1),
        [((2 * R, D), BF), unit, turn],
        [wide, unit, line, ((2 * R, R), BF)],
        flops=5 * step,
        name="far_texts",
        grant=GRANTS[2],
    )

    terms = (core.reshape(1), turn_i0, turn_i1, delta_i, turn_t0, turn_t2, delta_t0, delta_t2)
    (away,) = call(
        functools.partial(term_kernel, 1), terms, [((D, D), BF)], flops=2 * step, name="away", grant=GRANTS[3]
    )
    back = lax.ppermute(away, "dp", SWAP)
    (kept,) = call(
        functools.partial(term_kernel, 0), terms, [((D, D), F32)], flops=2 * step, name="kept", grant=GRANTS[4]
    )
    chip = (kept + back.astype(F32)).astype(BF).reshape(NY * NX, NZ * OWN, D)
    plane = lax.all_to_all(chip, "dp", 0, 0, axis_index_groups=PLANES, tiled=True)
    (plane,) = call(join_kernel, (plane,), [((2 * NZ, 5, D), BF)], name="join")
    column = lax.all_to_all(plane, "dp", 0, 0, axis_index_groups=COLUMNS, tiled=True)
    total = jnp.sum(column.astype(F32).reshape(NZ, 2, 5 * D), axis=0)
    mine = lax.dynamic_slice_in_dim(total, core * (D // 2), OWN * D // 2, 1)
    return mine[0], mine[1]


def solution(mesh):
    return jax.shard_map(
        local,
        mesh=mesh,
        in_specs=(P("dp", None), P("dp", None), P(), P(), P(), P(), P("dp")),
        out_specs=(P("dp"), P("dp")),
        check_vma=False,
    )
```

profile of v0, /device:TPU:1, one launch (start us, length us, event | category | flops | bytes accessed | tf_op | source)
XLA Modules:
  0.0 120.8 jit_solution(15329368509416913460)
XLA Ops:
  1.4 2.5 %broadcast_select_fusion.1.text = bf16[512,1152]{1,0:T(8,128)(2,1)} fusion(bf16[512,1152]{1,0:T(8,128)(2,1)} %param.8, pred[512]{0:T(512)(128)(4,1)S(1)} %iota_compare_fusion.1), kind=kLoop, calls=%fused_computation.4 | loop fusion | flops 589824 | bytes 2359808 | tf_op jit(solution)/shard_map/jit(_where)/select_n | solution.py:173
  3.9 1.2 %broadcast_select_fusion.image = bf16[512,1152]{1,0:T(8,128)(2,1)} fusion(bf16[512,1152]{1,0:T(8,128)(2,1)S(1)} %copy-done.3, pred[512]{0:T(512)(128)(4,1)S(1)} %iota_compare_fusion.1), kind=kLoop, calls=%fused_computation.3 | loop fusion | flops 589824 | bytes 2359808 | tf_op jit(solution)/shard_map/jit(_where)/select_n | solution.py:175
  5.1 3.2 %collective-permute-start = (bf16[512,1152]{1,0:T(8,128)(2,1)}, bf16[512,1152]{1,0:T(8,128)(2,1)}, u32[]{:S(2)}, u32[]{:S(2)}) collective-permute-start(bf16[512,1152]{1,0:T(8,128)(2,1)} %broadcast_select_fusion.image), channel_id=1, source_target_pairs={{0,255},{1,0},{2,1},{3,2},{4,3},{5,4},{6,5},{7,6},{8,7},{9,8},{10,... | collective-permute-start | bytes 3538952 | tf_op jit(solution)/shard_map/ppermute | solution.py:51
  8.4 0.0 collective-permute-start.1
  8.4 0.5 fusion.shuffle
  10.3 0.1 pad_maximum_fusion.scal
  10.3 1.7 %copy-done = bf16[1152,1152]{1,0:T(8,128)(2,1)S(1)} copy-done((bf16[1152,1152]{1,0:T(8,128)(2,1)S(1)}, bf16[1152,1152]{1,0:T(8,128)(2,1)}, u32[]{:S(2)}) %copy-start) | copy-done | bytes 2654232
  12.1 1.7 %copy-done.2 = bf16[1152,1152]{1,0:T(8,128)(2,1)S(1)} copy-done((bf16[1152,1152]{1,0:T(8,128)(2,1)S(1)}, bf16[1152,1152]{1,0:T(8,128)(2,1)}, u32[]{:S(2)}) %copy-start.2) | copy-done | bytes 2654232
  13.8 10.5 %own_rows.1 = (f32[512,1152]{1,0:T(8,128)S(1)}, bf16[512,1152]{1,0:T(8,128)(2,1)S(1)}, f32[512,1]{1,0:T(8,128)S(1)}, bf16[1152,512]{1,0:T(8,128)(2,1)S(1)}, f32[...) custom-call(f32[2]{0:T(128)S(1)} %pad_maximum_fusion.scal, ...), custom_call_target="tpu_custom_call" | custom-call | flops 6794772480 | bytes 22646792 | tf_op jit(solution)/shard_map/own_rows/pallas_call | solution.py:156
  24.4 8.5 %own_texts.1 = (f32[512,1152]{1,0:T(8,128)S(1)}, bf16[1024,1152]{1,0:T(8,128)(2,1)S(1)}, f32[512,1]{1,0:T(8,128)S(1)}, bf16[1152,512]{1,0:T(8,128)(2,1)S(1)}, f3...) custom-call(f32[2]{0:T(128)S(1)} %pad_maximum_fusion.scal, bf16[512,1152]{1,0:T(8,128)(2,1)} %collective-permute-done.image1, ...), custom_call_target="tpu_custom_call" | custom-call | flops 5435817984 | bytes 21172232 | tf_op jit(solution)/shard_map/own_texts/pallas_call | solution.py:156
  32.9 3.7 %collective-permute-done.1.text2 = bf16[512,1152]{1,0:T(8,128)(2,1)} collective-permute-done((bf16[512,1152]{1,0:T(8,128)(2,1)}, bf16[512,1152]{1,0:T(8,128)(2,1)}, u32[]{:S(2)}, u32[]{:S(2)}) %collective-permute-start.1) | collective-permute-done | bytes 1179680 | tf_op jit(solution)/shard_map/ppermute | solution.py:51
  36.6 10.5 %far_texts.1 = (bf16[1024,1152]{1,0:T(8,128)(2,1)S(1)}, bf16[512,1152]{1,0:T(8,128)(2,1)S(1)}, bf16[1152,512]{1,0:T(8,128)(2,1)S(1)}) custom-call(f32[2]{0:T(128)S(1)} %pad_maximum_fusion.scal, bf16[512,1152]{1,0:T(8,128)(2,1)} %collective-permute-done.1.text2, bf16[1152,1152]{1,0:T(8,128)(2,1)S(1)} %copy-done.2, bf16[1152,1152]{1,0:T(8,128)(2,1)S(1)} %fusion.shuffle, ...), custom_call_target="tpu_custom_call" | custom-call | flops 6794772480 | bytes 23007240 | tf_op jit(solution)/shard_map/far_texts/pallas_call | solution.py:156
  47.1 3.6 %away.1 = bf16[1152,1152]{1,0:T(8,128)(2,1)S(1)} custom-call(s32[1]{0:T(128)} %bitcast.which, bf16[1152,512]{1,0:T(8,128)(2,1)S(1)} %get-tuple-element.25.turn_i0, bf16[1152,512]{1,0:T(8,128)(2,1)S(1)} %get-tuple-element.31.turn_i1, bf16[1024,1152]{1,0:T(8,128)(2,1)S(1)} %get-tuple-element.39.delta_i, bf16[1152,512]{1,0:T(8,128)(2,1)S(1)} %get-tuple-element.40.turn_t0, ...), custom_call_target="tpu_custom_call" | custom-call | flops 2717908992 | bytes 12091396 | tf_op jit(solution)/shard_map/away/pallas_call | solution.py:156
  50.7 7.6 %collective-permute-start.2 = (bf16[1152,1152]{1,0:T(8,128)(2,1)S(1)}, bf16[1152,1152]{1,0:T(8,128)(2,1)S(1)}, u32[]{:S(2)}, u32[]{:S(2)}) collective-permute-start(bf16[1152,1152]{1,0:T(8,128)(2,1)S(1)} %away.1), channel_id=1, source_target_pairs={{0,1},{1,0},{2,3},{3,2},{4,5},{5,4},{6,7},{7,6},{8,9},{9,8},{10,11... | collective-permute-start | bytes 7962632 | tf_op jit(solution)/shard_map/ppermute | solution.py:215
  58.3 3.5 %kept.1 = f32[1152,1152]{1,0:T(8,128)S(1)} custom-call(s32[1]{0:T(128)} %bitcast.which, bf16[1152,512]{1,0:T(8,128)(2,1)S(1)} %get-tuple-element.25.turn_i0, bf16[1152,512]{1,0:T(8,128)(2,1)S(1)} %get-tuple-element.31.turn_i1, bf16[1024,1152]{1,0:T(8,128)(2,1)S(1)} %get-tuple-element.39.delta_i, bf16[1152,512]{1,0:T(8,128)(2,1)S(1)} %get-tuple-element.40.turn_t0, ...), custom_call_target="tpu_custom_call" | custom-call | flops 2717908992 | bytes 14745604 | tf_op jit(solution)/shard_map/kept/pallas_call | solution.py:156
  61.9 1.0 collective-permute-done.2
  62.9 0.6 add_convert_fusion
  63.5 36.6 %all_to_all.10.plane = bf16[16,72,1152]{2,1,0:T(8,128)(2,1)S(1)} all-to-all(bf16[16,72,1152]{2,1,0:T(8,128)(2,1)S(1)} %bitcast.3), channel_id=1, replica_groups={{0,2,4,6,64,66,68,70,128,130,132,134,192,194,196,198},{1,3,5,7,65,67,69..., dimensions={0} | all-to-all | bytes 5308416 | tf_op jit(solution)/shard_map/all_to_all | solution.py:220
  100.1 1.1 join.1
  101.2 6.0 %all-to-all-start.1 = ((bf16[16,5,1152]{2,1,0:T(8,128)(2,1)}), bf16[16,5,1152]{2,1,0:T(8,128)(2,1)S(1)}, u32[]{:S(2)}, u32[]{:S(2)}) async-start(bf16[16,5,1152]{2,1,0:T(8,128)(2,1)} %join.1), calls=%async_computation.1 | async-start | bytes 589824 | tf_op jit(solution)/shard_map/all_to_all | solution.py:222
  107.3 12.4 %all-to-all-done.1 = bf16[16,5,1152]{2,1,0:T(8,128)(2,1)S(1)} async-done(((bf16[16,5,1152]{2,1,0:T(8,128)(2,1)}), bf16[16,5,1152]{2,1,0:T(8,128)(2,1)S(1)}, u32[]{:S(2)}, u32[]{:S(2)}) %all-to-all-start.1) | async-done | bytes 184352 | tf_op jit(solution)/shard_map/all_to_all | solution.py:222
  119.6 0.3 reshape.26
  119.9 0.1 reduce_sum.9
  120.0 0.8 dynamic-slice_reduce_fusion
  (10 shorter events, 0.1 us)
Async XLA Ops:
  0.6 3.3 %copy-start.3 = (bf16[512,1152]{1,0:T(8,128)(2,1)S(1)}, bf16[512,1152]{1,0:T(8,128)(2,1)}, u32[]{:S(2)}) copy-start(bf16[512,1152]{1,0:T(8,128)(2,1)} %param.7) | copy-start | bytes 3538948
  5.1 19.3 %collective-permute-start = (bf16[512,1152]{1,0:T(8,128)(2,1)}, bf16[512,1152]{1,0:T(8,128)(2,1)}, u32[]{:S(2)}, u32[]{:S(2)}) collective-permute-start(bf16[512,1152]{1,0:T(8,128)(2,1)} %broadcast_select_fusion.image), channel_id=1, source_target_pairs={{0,255},{1,0},{2,1},{3,2},{4,3},{5,4},{6,5},{7,6},{8,7},{9,8},{10,... | collective-permute-start | bytes 3538952 | tf_op jit(solution)/shard_map/ppermute | solution.py:51
  8.4 28.2 %collective-permute-start.1 = (bf16[512,1152]{1,0:T(8,128)(2,1)}, bf16[512,1152]{1,0:T(8,128)(2,1)}, u32[]{:S(2)}, u32[]{:S(2)}) collective-permute-start(bf16[512,1152]{1,0:T(8,128)(2,1)} %broadcast_select_fusion.1.text), channel_id=1, source_target_pairs={{0,2},{1,3},{2,4},{3,5},{4,6},{5,7},{6,8},{7,9},{8,10},{9,11},{10,... | collective-permute-start | bytes 3538952 | tf_op jit(solution)/shard_map/ppermute | solution.py:51
  10.3 1.8 %copy-start = (bf16[1152,1152]{1,0:T(8,128)(2,1)S(1)}, bf16[1152,1152]{1,0:T(8,128)(2,1)}, u32[]{:S(2)}) copy-start(bf16[1152,1152]{1,0:T(8,128)(2,1)} %image_proj.3) | copy-start | bytes 7962628
  12.1 1.7 %copy-start.2 = (bf16[1152,1152]{1,0:T(8,128)(2,1)S(1)}, bf16[1152,1152]{1,0:T(8,128)(2,1)}, u32[]{:S(2)}) copy-start(bf16[1152,1152]{1,0:T(8,128)(2,1)} %text_proj.3) | copy-start | bytes 7962628
  13.8 10.6 %copy-start.1 = (bf16[1152,1152]{1,0:T(8,128)(2,1)S(1)}, bf16[1152,1152]{1,0:T(8,128)(2,1)}, u32[]{:S(2)}) copy-start(bf16[1152,1152]{1,0:T(8,128)(2,1)} %image_proj.3) | copy-start | bytes 7962628
  50.7 12.2 %collective-permute-start.2 = (bf16[1152,1152]{1,0:T(8,128)(2,1)S(1)}, bf16[1152,1152]{1,0:T(8,128)(2,1)S(1)}, u32[]{:S(2)}, u32[]{:S(2)}) collective-permute-start(bf16[1152,1152]{1,0:T(8,128)(2,1)S(1)} %away.1), channel_id=1, source_target_pairs={{0,1},{1,0},{2,3},{3,2},{4,5},{5,4},{6,7},{7,6},{8,9},{9,8},{10,11... | collective-permute-start | bytes 7962632 | tf_op jit(solution)/shard_map/ppermute | solution.py:215
  101.2 18.4 %all-to-all-start.1 = ((bf16[16,5,1152]{2,1,0:T(8,128)(2,1)}), bf16[16,5,1152]{2,1,0:T(8,128)(2,1)S(1)}, u32[]{:S(2)}, u32[]{:S(2)}) async-start(bf16[16,5,1152]{2,1,0:T(8,128)(2,1)} %join.1), calls=%async_computation.1 | async-start | bytes 589824 | tf_op jit(solution)/shard_map/all_to_all | solution.py:222
where the time goes:
time: 121 us
  Pallas kernels  37.8 us (31%)
  blocking collectives  36.6 us (30%)
  waiting for transfers between devices  17.1 us (14%)
  starting transfers between devices  16.9 us (14%)
  other arithmetic  5.05 us (4%)
  local copies, waits for them, and re-layouts  4.56 us (4%)
  between operations  2.81 us (2%)
    pallas_call x6, Pallas kernels, call(): pl.pallas_call(kernel, out_shape=shapes, in_specs=[SMEM if a.size < 8 els...  37.8 us
    all_to_all x1, blocking collectives, local(): lax.all_to_all(chip, 'dp', 0, 0, axis_index_groups=PLANES, tiled=True)  36.6 us
    all_to_all x1, waiting for transfers between devices, local(): lax.all_to_all(plane, 'dp', 0, 0, axis_index_groups=COLUMNS, tiled=True)  12.4 us
    ppermute x1, starting transfers between devices, local(): back = lax.ppermute(away, 'dp', SWAP)  7.63 us
    all_to_all x1, starting transfers between devices, local(): lax.all_to_all(plane, 'dp', 0, 0, axis_index_groups=COLUMNS, tiled=True)  6.02 us
    ppermute x2, waiting for transfers between devices, shift(): return lax.ppermute(value, 'dp', [(d, (d + steps) % N) for d in range(N)])  3.69 us
    unnamed x8, local copies, waits for them, and re-layouts  3.51 us
    ppermute x2, starting transfers between devices, shift(): return lax.ppermute(value, 'dp', [(d, (d + steps) % N) for d in range(N)])  3.24 us
  transfers between devices with their start and end apart: 4, of which 3 were waited for; matrix products, arithmetic and copies ran while one was open for 1% of the time, Pallas kernels for 19%

commit v1 on v0

--- a/solution.py
+++ b/solution.py
@@ -14,11 +14,12 @@
 NY, NZ, NX = 4, 8, 4
 N = 256
 OWN = 9
-PART = 384
+PART = 576
 GRANTS = (10,10,12,10,10)
 BF = jnp.bfloat16
 F32 = jnp.float32
 VMEM = pl.BlockSpec(memory_space=pltpu.VMEM)
+ANY = pl.BlockSpec(memory_space=pl.ANY)
 SMEM = pl.BlockSpec(memory_space=pltpu.SMEM)
 
 
@@ -81,6 +82,25 @@
 def raw_grad(gradient, direction, inverse):
     radial = jnp.sum(direction * gradient, axis=1, keepdims=True)
     return ((gradient - direction * radial) * inverse).astype(BF)
+
+
+def live_kernel(count, text, image, text0, image0, zero, sem):
+    zero[...] = jnp.zeros_like(zero)
+    for a, (source, target) in enumerate(((text, text0), (image, image0))):
+        for k in range(R // BLK):
+            rows = slice(k * BLK, (k + 1) * BLK)
+
+            @pl.when(k < count[0])
+            def _():
+                pltpu.make_async_copy(source.at[rows], target.at[rows], sem.at[a, k]).start()
+
+            @pl.when(k >= count[0])
+            def _():
+                pltpu.make_async_copy(zero, target.at[rows], sem.at[a, k]).start()
+
+    for a, target in enumerate((text0, image0)):
+        for k in range(R // BLK):
+            pltpu.make_async_copy(zero, target.at[k * BLK:(k + 1) * BLK], sem.at[a, k]).wait()
 
 
 def first_kernel(scal, text, image, text_proj, image_proj, shuffle,
@@ -142,11 +162,18 @@
         total(turn_t0, turn_t2, delta_t0, delta_t2)
 
 
-def join_kernel(plane, out):
+def join_kernel(plane, out, packed):
     total = jnp.sum(plane[...].astype(F32), axis=0)
+    packed[...] = jnp.zeros_like(packed)
     for z in range(NZ):
         for h in range(2):
-            out[2 * z + h] = total[OWN * z + 4 * h:OWN * z + 4 * h + 5, :].astype(BF)
+            k, top, middle, lane = 2 * z + h, OWN * z + 5 * h, OWN * z + 4, 512 * h
+            packed[k, 0:4, 0:640] = total[top:top + 4, 0:640]
+            packed[k, 4:8, 0:512] = total[top:top + 4, 640:D]
+            packed[k, 4:5, 512:768] = total[middle:middle + 1, lane:lane + 256]
+            packed[k, 5:6, 512:768] = total[middle:middle + 1, lane + 256:lane + 512]
+            packed[k, 6:7, 512:640] = total[middle:middle + 1, lane + 512:lane + 640]
+    out[...] = packed[...].astype(BF)
 
 
 def call(kernel, operands, outs, scratch=(), flops=0, name=None, grant=8):
@@ -167,12 +194,15 @@
 
 def local(image_feat, text_feat, image_proj, text_proj, logit_scale_logarithm, bias, counts):
     scal = jnp.stack([jnp.exp(logit_scale_logarithm[0]), bias[0]])
-    rows = lax.broadcasted_iota(jnp.int32, image_feat.shape, 0)
-    live = rows < counts[0] * BLK
-    zero = jnp.zeros((), BF)
-    text0 = jnp.where(live, text_feat, zero)
-    image_feat, text0 = lax.optimization_barrier((image_feat, text0))
-    image0 = jnp.where(live, image_feat, zero)
+    text0, image0 = pl.pallas_call(
+        live_kernel,
+        out_shape=[jax.ShapeDtypeStruct((R, D), BF)] * 2,
+        in_specs=[SMEM, ANY, ANY],
+        out_specs=[ANY, ANY],
+        scratch_shapes=[pltpu.VMEM((BLK, D), BF), pltpu.SemaphoreType.DMA((2, R // BLK))],
+        compiler_params=pltpu.CompilerParams(vmem_limit_bytes=58 << 20),
+        name="live_rows",
+    )(counts, text_feat, image_feat)
     text2 = shift(text0, 2)
     image1 = shift(image0, -1)
     shuffle = shuffle_matrix()
@@ -218,10 +248,15 @@
     )
     chip = (kept + back.astype(F32)).astype(BF).reshape(NY * NX, NZ * OWN, D)
     plane = lax.all_to_all(chip, "dp", 0, 0, axis_index_groups=PLANES, tiled=True)
-    (plane,) = call(join_kernel, (plane,), [((2 * NZ, 5, D), BF)], name="join")
+    (plane,) = call(
+        join_kernel, (plane,), [((2 * NZ, 8, 768), BF)], [((2 * NZ, 8, 768), F32)], name="join"
+    )
     column = lax.all_to_all(plane, "dp", 0, 0, axis_index_groups=COLUMNS, tiled=True)
-    total = jnp.sum(column.astype(F32).reshape(NZ, 2, 5 * D), axis=0)
-    mine = lax.dynamic_slice_in_dim(total, core * (D // 2), OWN * D // 2, 1)
+    total = jnp.sum(column.astype(F32).reshape(NZ, 2, 8, 768), axis=0)
+    four = jnp.concatenate([total[:, :4, :640], total[:, 4:, :512]], axis=2).reshape(2, 4 * D)
+    middle = total[:, 4:7, 512:].reshape(2, 768)[:, :640]
+    whole = jnp.concatenate([middle, four, middle], axis=1)
+    mine = lax.dynamic_slice_in_dim(whole, jnp.where(core == 0, 640, 64), OWN * D // 2, 1)
     return mine[0], mine[1]
 
 

time: 121 us -> 186 us (1.54)
  Pallas kernels: 37.8 us -> 109 us
  blocking collectives: 36.6 us -> 44.9 us
  starting transfers between devices: 16.9 us -> 9.8 us
  waiting for transfers between devices: 17.1 us -> 11.6 us
  other arithmetic: 5.05 us -> 1.44 us
  local copies, waits for them, and re-layouts: 4.56 us -> 6.8 us
    pallas_call x0 -> x1, Pallas kernels: none -> 72.7 us  [local(): pl.pallas_call(live_kernel, out_shape=[jax.ShapeDtypeStruct((R, D), BF)]...]
    all_to_all x1, blocking collectives: 36.6 us -> 44.9 us  [local(): lax.all_to_all(chip, 'dp', 0, 0, axis_index_groups=PLANES, tiled=True)]
    ppermute x1, starting transfers between devices: 7.63 us -> 0.9 us  [local(): back = lax.ppermute(away, 'dp', SWAP)]
    select_n x2 -> x0, other arithmetic: 3.73 us -> none  [the longest x1 2.5 us: local(): text0 = jnp.where(live, text_feat, zero)]
    ppermute x2, waiting for transfers between devices: 3.69 us -> 0.15 us  [shift(): return lax.ppermute(value, 'dp', [(d, (d + steps) % N) for d in range(N)])]
    unnamed x8 -> x13, local copies, waits for them, and re-layouts: 3.51 us -> 6.07 us
    all_to_all x1, waiting for transfers between devices: 12.4 us -> 10.3 us  [local(): lax.all_to_all(plane, 'dp', 0, 0, axis_index_groups=COLUMNS, tiled=True)]
  transfers between devices with their start and end apart: 4 -> 4, of which waited for: 3 -> 3; matrix products, arithmetic and copies ran while one was open for 1% -> 0% of each run, Pallas kernels for 19% -> 11%
where the time goes in v1:
time: 186 us
  Pallas kernels  109 us (59%)
  blocking collectives  44.9 us (24%)
  waiting for transfers between devices  11.6 us (6%)
  starting transfers between devices  9.8 us (5%)
  local copies, waits for them, and re-layouts  6.8 us (4%)
  between operations  2.75 us (1%)
    pallas_call x1, Pallas kernels, local(): pl.pallas_call(live_kernel, out_shape=[jax.ShapeDtypeStruct((R, D), BF)]...  72.7 us
    all_to_all x1, blocking collectives, local(): lax.all_to_all(chip, 'dp', 0, 0, axis_index_groups=PLANES, tiled=True)  44.9 us
    pallas_call x6, Pallas kernels, call(): pl.pallas_call(kernel, out_shape=shapes, in_specs=[SMEM if a.size < 8 els...  36.4 us
    all_to_all x1, waiting for transfers between devices, local(): lax.all_to_all(plane, 'dp', 0, 0, axis_index_groups=COLUMNS, tiled=True)  10.3 us
    all_to_all x1, starting transfers between devices, local(): lax.all_to_all(plane, 'dp', 0, 0, axis_index_groups=COLUMNS, tiled=True)  6.7 us
    unnamed x13, local copies, waits for them, and re-layouts  6.07 us
  transfers between devices with their start and end apart: 4, of which 3 were waited for; matrix products, arithmetic and copies ran while one was open for 0% of the time, Pallas kernels for 11%

profile of v1, /device:TPU:1, one launch (start us, length us, event | category | flops | bytes accessed | tf_op | source)
XLA Modules:
  0.0 186.4 jit_solution(1038732946247605325)
XLA Ops:
  1.3 72.7 %live_rows.1 = (bf16[512,1152]{1,0:T(8,128)(2,1)}, bf16[512,1152]{1,0:T(8,128)(2,1)}) custom-call(s32[1]{0:T(128)S(6)} %copy.13.count, bf16[512,1152]{1,0:T(8,128)(2,1)} %text.1, bf16[512,1152]{1,0:T(8,128)(2,1)} %image.1), custom_call_target="tpu_custom_call" | custom-call | tf_op jit(solution)/shard_map/live_rows/pallas_call | solution.py:197
  73.9 0.1 collective-permute-start
  74.0 2.1 %collective-permute-start.1 = (bf16[512,1152]{1,0:T(8,128)(2,1)}, bf16[512,1152]{1,0:T(8,128)(2,1)}, u32[]{:S(2)}, u32[]{:S(2)}) collective-permute-start(bf16[512,1152]{1,0:T(8,128)(2,1)} %get-tuple-element.23.text), channel_id=1, source_target_pairs={{0,2},{1,3},{2,4},{3,5},{4,6},{5,7},{6,8},{7,9},{8,10},{9,11},{10,... | collective-permute-start | bytes 3538952 | tf_op jit(solution)/shard_map/ppermute | solution.py:52
  76.2 0.5 fusion.shuffle
  78.0 0.1 pad_maximum_fusion.scal
  78.1 1.7 copy-done
  79.9 1.7 copy-done.2
  81.6 1.3 copy-done.3
  82.9 1.3 copy-done.4
  84.2 9.3 %own_rows.1 = (f32[512,1152]{1,0:T(8,128)S(1)}, bf16[512,1152]{1,0:T(8,128)(2,1)S(1)}, f32[512,1]{1,0:T(8,128)S(1)}, bf16[1152,512]{1,0:T(8,128)(2,1)S(1)}, f32[...) custom-call(f32[2]{0:T(128)S(1)} %pad_maximum_fusion.scal, ...), custom_call_target="tpu_custom_call" | custom-call | flops 6794772480 | bytes 22646792 | tf_op jit(solution)/shard_map/own_rows/pallas_call | solution.py:183
  93.5 8.4 %own_texts.1 = (f32[512,1152]{1,0:T(8,128)S(1)}, bf16[1024,1152]{1,0:T(8,128)(2,1)S(1)}, f32[512,1]{1,0:T(8,128)S(1)}, bf16[1152,512]{1,0:T(8,128)(2,1)S(1)}, f3...) custom-call(f32[2]{0:T(128)S(1)} %pad_maximum_fusion.scal, bf16[512,1152]{1,0:T(8,128)(2,1)} %collective-permute-done.image1, ...), custom_call_target="tpu_custom_call" | custom-call | flops 5435817984 | bytes 21172232 | tf_op jit(solution)/shard_map/own_texts/pallas_call | solution.py:183
  101.9 0.1 collective-permute-done.1.text2
  102.1 10.6 %far_texts.1 = (bf16[1024,1152]{1,0:T(8,128)(2,1)S(1)}, bf16[512,1152]{1,0:T(8,128)(2,1)S(1)}, bf16[1152,512]{1,0:T(8,128)(2,1)S(1)}) custom-call(f32[2]{0:T(128)S(1)} %pad_maximum_fusion.scal, bf16[512,1152]{1,0:T(8,128)(2,1)} %collective-permute-done.1.text2, bf16[1152,1152]{1,0:T(8,128)(2,1)S(1)} %copy-done.2, bf16[1152,1152]{1,0:T(8,128)(2,1)S(1)} %fusion.shuffle, ...), custom_call_target="tpu_custom_call" | custom-call | flops 6794772480 | bytes 23007240 | tf_op jit(solution)/shard_map/far_texts/pallas_call | solution.py:183
  112.6 3.4 %away.1 = bf16[1152,1152]{1,0:T(8,128)(2,1)S(1)} custom-call(s32[1]{0:T(128)} %bitcast.which, bf16[1152,512]{1,0:T(8,128)(2,1)S(1)} %get-tuple-element.25.turn_i0, bf16[1152,512]{1,0:T(8,128)(2,1)S(1)} %get-tuple-element.31.turn_i1, bf16[1024,1152]{1,0:T(8,128)(2,1)S(1)} %get-tuple-element.39.delta_i, bf16[1152,512]{1,0:T(8,128)(2,1)S(1)} %get-tuple-element.40.turn_t0, ...), custom_call_target="tpu_custom_call" | custom-call | flops 2717908992 | bytes 12091396 | tf_op jit(solution)/shard_map/away/pallas_call | solution.py:183
  116.1 0.9 collective-permute-start.2
  117.0 3.4 %kept.1 = f32[1152,1152]{1,0:T(8,128)S(1)} custom-call(s32[1]{0:T(128)} %bitcast.which, bf16[1152,512]{1,0:T(8,128)(2,1)S(1)} %get-tuple-element.25.turn_i0, bf16[1152,512]{1,0:T(8,128)(2,1)S(1)} %get-tuple-element.31.turn_i1, bf16[1024,1152]{1,0:T(8,128)(2,1)S(1)} %get-tuple-element.39.delta_i, bf16[1152,512]{1,0:T(8,128)(2,1)S(1)} %get-tuple-element.40.turn_t0, ...), custom_call_target="tpu_custom_call" | custom-call | flops 2717908992 | bytes 14745604 | tf_op jit(solution)/shard_map/kept/pallas_call | solution.py:183
  120.4 1.2 collective-permute-done.2
  121.5 0.6 add_convert_fusion
  122.1 44.9 %all_to_all.10.plane = bf16[16,72,1152]{2,1,0:T(8,128)(2,1)S(1)} all-to-all(bf16[16,72,1152]{2,1,0:T(8,128)(2,1)S(1)} %bitcast.10), channel_id=1, replica_groups={{0,2,4,6,64,66,68,70,128,130,132,134,192,194,196,198},{1,3,5,7,65,67,69..., dimensions={0} | all-to-all | bytes 5308416 | tf_op jit(solution)/shard_map/all_to_all | solution.py:250
  167.0 1.3 join.1
  168.3 6.7 %all-to-all-start.1 = ((bf16[16,8,768]{2,1,0:T(8,128)(2,1)}), bf16[16,8,768]{2,1,0:T(8,128)(2,1)S(1)}, u32[]{:S(2)}, u32[]{:S(2)}) async-start(bf16[16,8,768]{2,1,0:T(8,128)(2,1)} %join.1), calls=%async_computation.1 | async-start | bytes 393216 | tf_op jit(solution)/shard_map/all_to_all | solution.py:254
  175.0 10.3 %all-to-all-done.1 = bf16[16,8,768]{2,1,0:T(8,128)(2,1)S(1)} async-done(((bf16[16,8,768]{2,1,0:T(8,128)(2,1)}), bf16[16,8,768]{2,1,0:T(8,128)(2,1)S(1)}, u32[]{:S(2)}, u32[]{:S(2)}) %all-to-all-start.1) | async-done | bytes 196640 | tf_op jit(solution)/shard_map/all_to_all | solution.py:254
  185.5 0.2 fusion.2
  185.7 0.7 slice_reduce_fusion
  (17 shorter events, 0.1 us)
Async XLA Ops:
  73.9 19.5 %collective-permute-start = (bf16[512,1152]{1,0:T(8,128)(2,1)}, bf16[512,1152]{1,0:T(8,128)(2,1)}, u32[]{:S(2)}, u32[]{:S(2)}) collective-permute-start(bf16[512,1152]{1,0:T(8,128)(2,1)} %get-tuple-element.24.image), channel_id=1, source_target_pairs={{0,255},{1,0},{2,1},{3,2},{4,3},{5,4},{6,5},{7,6},{8,7},{9,8},{10,... | collective-permute-start | bytes 3538952 | tf_op jit(solution)/shard_map/ppermute | solution.py:52
  74.0 28.0 %collective-permute-start.1 = (bf16[512,1152]{1,0:T(8,128)(2,1)}, bf16[512,1152]{1,0:T(8,128)(2,1)}, u32[]{:S(2)}, u32[]{:S(2)}) collective-permute-start(bf16[512,1152]{1,0:T(8,128)(2,1)} %get-tuple-element.23.text), channel_id=1, source_target_pairs={{0,2},{1,3},{2,4},{3,5},{4,6},{5,7},{6,8},{7,9},{8,10},{9,11},{10,... | collective-permute-start | bytes 3538952 | tf_op jit(solution)/shard_map/ppermute | solution.py:52
  78.1 1.8 copy-start
  79.9 1.7 copy-start.2
  81.6 1.3 copy-start.3
  82.9 1.3 copy-start.4
  84.2 9.3 %copy-start.1 = (bf16[1152,1152]{1,0:T(8,128)(2,1)S(1)}, bf16[1152,1152]{1,0:T(8,128)(2,1)}, u32[]{:S(2)}) copy-start(bf16[1152,1152]{1,0:T(8,128)(2,1)} %image_proj.3) | copy-start | bytes 7962628
  116.1 5.5 %collective-permute-start.2 = (bf16[1152,1152]{1,0:T(8,128)(2,1)S(1)}, bf16[1152,1152]{1,0:T(8,128)(2,1)S(1)}, u32[]{:S(2)}, u32[]{:S(2)}) collective-permute-start(bf16[1152,1152]{1,0:T(8,128)(2,1)S(1)} %away.1), channel_id=1, source_target_pairs={{0,1},{1,0},{2,3},{3,2},{4,5},{5,4},{6,7},{7,6},{8,9},{9,8},{10,11... | collective-permute-start | bytes 7962632 | tf_op jit(solution)/shard_map/ppermute | solution.py:245
  168.3 17.0 %all-to-all-start.1 = ((bf16[16,8,768]{2,1,0:T(8,128)(2,1)}), bf16[16,8,768]{2,1,0:T(8,128)(2,1)S(1)}, u32[]{:S(2)}, u32[]{:S(2)}) async-start(bf16[16,8,768]{2,1,0:T(8,128)(2,1)} %join.1), calls=%async_computation.1 | async-start | bytes 393216 | tf_op jit(solution)/shard_map/all_to_all | solution.py:254

commit v2 on v1

--- a/solution.py
+++ b/solution.py
@@ -84,23 +84,29 @@
     return ((gradient - direction * radial) * inverse).astype(BF)
 
 
-def live_kernel(count, text, image, text0, image0, zero, sem):
-    zero[...] = jnp.zeros_like(zero)
-    for a, (source, target) in enumerate(((text, text0), (image, image0))):
-        for k in range(R // BLK):
-            rows = slice(k * BLK, (k + 1) * BLK)
-
+def live_kernel(count, text, image, text0, image0, held, sem):
+    jobs = ((text, text0), (image, image0))
+    blocks = [slice(k * BLK, (k + 1) * BLK) for k in range(R // BLK)]
+    for a, (source, _) in enumerate(jobs):
+        for k, rows in enumerate(blocks):
             @pl.when(k < count[0])
             def _():
-                pltpu.make_async_copy(source.at[rows], target.at[rows], sem.at[a, k]).start()
+                pltpu.make_async_copy(source.at[rows], held.at[a, rows], sem.at[0, a, k]).start()
 
             @pl.when(k >= count[0])
             def _():
-                pltpu.make_async_copy(zero, target.at[rows], sem.at[a, k]).start()
-
-    for a, target in enumerate((text0, image0)):
-        for k in range(R // BLK):
-            pltpu.make_async_copy(zero, target.at[k * BLK:(k + 1) * BLK], sem.at[a, k]).wait()
+                held[a, rows] = jnp.zeros((BLK, D), BF)
+
+    for a, (source, target) in enumerate(jobs):
+        for k, rows in enumerate(blocks):
+            @pl.when(k < count[0])
+            def _():
+                pltpu.make_async_copy(source.at[rows], held.at[a, rows], sem.at[0, a, k]).wait()
+
+            pltpu.make_async_copy(held.at[a, rows], target.at[rows], sem.at[1, a, k]).start()
+    for a, (_, target) in enumerate(jobs):
+        for k, rows in enumerate(blocks):
+            pltpu.make_async_copy(held.at[a, rows], target.at[rows], sem.at[1, a, k]).wait()
 
 
 def first_kernel(scal, text, image, text_proj, image_proj, shuffle,
@@ -199,7 +205,7 @@
         out_shape=[jax.ShapeDtypeStruct((R, D), BF)] * 2,
         in_specs=[SMEM, ANY, ANY],
         out_specs=[ANY, ANY],
-        scratch_shapes=[pltpu.VMEM((BLK, D), BF), pltpu.SemaphoreType.DMA((2, R // BLK))],
+        scratch_shapes=[pltpu.VMEM((2, R, D), BF), pltpu.SemaphoreType.DMA((2, 2, R // BLK))],
         compiler_params=pltpu.CompilerParams(vmem_limit_bytes=58 << 20),
         name="live_rows",
     )(counts, text_feat, image_feat)

time: 186 us -> 119 us (0.64)
  Pallas kernels: 109 us -> 38.9 us
  starting transfers between devices: 9.8 us -> 18.5 us
  blocking collectives: 44.9 us -> 36.6 us
  waiting for transfers between devices: 11.6 us -> 13.9 us
    pallas_call x1, Pallas kernels: 72.7 us -> 2.51 us  [local(): pl.pallas_call(live_kernel, out_shape=[jax.ShapeDtypeStruct((R, D), BF)]...]
    all_to_all x1, blocking collectives: 44.9 us -> 36.6 us  [local(): lax.all_to_all(chip, 'dp', 0, 0, axis_index_groups=PLANES, tiled=True)]
    ppermute x1, starting transfers between devices: 0.9 us -> 7.84 us  [local(): back = lax.ppermute(away, 'dp', SWAP)]
    ppermute x2, waiting for transfers between devices: 0.15 us -> 2.41 us  [shift(): return lax.ppermute(value, 'dp', [(d, (d + steps) % N) for d in range(N)])]
  transfers between devices with their start and end apart: 4 -> 4, of which waited for: 3 -> 3; matrix products, arithmetic and copies ran while one was open for 0% -> 1% of each run, Pallas kernels for 11% -> 18%
where the time goes in v2:
time: 119 us
  Pallas kernels  38.9 us (33%)
  blocking collectives  36.6 us (31%)
  starting transfers between devices  18.5 us (16%)
  waiting for transfers between devices  13.9 us (12%)
  local copies, waits for them, and re-layouts  6.8 us (6%)
  between operations  2.75 us (2%)
  other arithmetic  1.44 us (1%)
    all_to_all x1, blocking collectives, local(): lax.all_to_all(chip, 'dp', 0, 0, axis_index_groups=PLANES, tiled=True)  36.6 us
    pallas_call x6, Pallas kernels, call(): pl.pallas_call(kernel, out_shape=shapes, in_specs=[SMEM if a.size < 8 els...  36.4 us
    all_to_all x1, waiting for transfers between devices, local(): lax.all_to_all(plane, 'dp', 0, 0, axis_index_groups=COLUMNS, tiled=True)  10.3 us
    ppermute x1, starting transfers between devices, local(): back = lax.ppermute(away, 'dp', SWAP)  7.84 us
    all_to_all x1, starting transfers between devices, local(): lax.all_to_all(plane, 'dp', 0, 0, axis_index_groups=COLUMNS, tiled=True)  7.31 us
    unnamed x13, local copies, waits for them, and re-layouts  6.07 us
    ppermute x2, starting transfers between devices, shift(): return lax.ppermute(value, 'dp', [(d, (d + steps) % N) for d in range(N)])  3.32 us
    pallas_call x1, Pallas kernels, local(): pl.pallas_call(live_kernel, out_shape=[jax.ShapeDtypeStruct((R, D), BF)]...  2.51 us
  transfers between devices with their start and end apart: 4, of which 3 were waited for; matrix products, arithmetic and copies ran while one was open for 1% of the time, Pallas kernels for 18%

profile of v2, /device:TPU:1, one launch (start us, length us, event | category | flops | bytes accessed | tf_op | source)
XLA Modules:
  0.0 118.9 jit_solution(14941663388001863128)
XLA Ops:
  1.3 2.5 %live_rows.1 = (bf16[512,1152]{1,0:T(8,128)(2,1)}, bf16[512,1152]{1,0:T(8,128)(2,1)}) custom-call(s32[1]{0:T(128)S(6)} %copy.13.count, bf16[512,1152]{1,0:T(8,128)(2,1)} %text.1, bf16[512,1152]{1,0:T(8,128)(2,1)} %image.1), custom_call_target="tpu_custom_call" | custom-call | tf_op jit(solution)/shard_map/live_rows/pallas_call | solution.py:203
  3.8 3.3 %collective-permute-start = (bf16[512,1152]{1,0:T(8,128)(2,1)}, bf16[512,1152]{1,0:T(8,128)(2,1)}, u32[]{:S(2)}, u32[]{:S(2)}) collective-permute-start(bf16[512,1152]{1,0:T(8,128)(2,1)} %get-tuple-element.24.image), channel_id=1, source_target_pairs={{0,255},{1,0},{2,1},{3,2},{4,3},{5,4},{6,5},{7,6},{8,7},{9,8},{10,... | collective-permute-start | bytes 3538952 | tf_op jit(solution)/shard_map/ppermute | solution.py:52
  7.1 0.0 collective-permute-start.1
  7.2 0.5 fusion.shuffle
  9.0 0.1 pad_maximum_fusion.scal
  9.1 1.7 %copy-done = bf16[1152,1152]{1,0:T(8,128)(2,1)S(1)} copy-done((bf16[1152,1152]{1,0:T(8,128)(2,1)S(1)}, bf16[1152,1152]{1,0:T(8,128)(2,1)}, u32[]{:S(2)}) %copy-start) | copy-done | bytes 2654232
  10.8 1.7 %copy-done.2 = bf16[1152,1152]{1,0:T(8,128)(2,1)S(1)} copy-done((bf16[1152,1152]{1,0:T(8,128)(2,1)S(1)}, bf16[1152,1152]{1,0:T(8,128)(2,1)}, u32[]{:S(2)}) %copy-start.2) | copy-done | bytes 2654232
  12.6 1.3 %copy-done.3 = bf16[512,1152]{1,0:T(8,128)(2,1)S(1)} copy-done((bf16[512,1152]{1,0:T(8,128)(2,1)S(1)}, bf16[512,1152]{1,0:T(8,128)(2,1)}, u32[]{:S(2)}) %copy-start.3) | copy-done | bytes 1179672
  13.9 1.3 %copy-done.4 = bf16[512,1152]{1,0:T(8,128)(2,1)S(1)} copy-done((bf16[512,1152]{1,0:T(8,128)(2,1)S(1)}, bf16[512,1152]{1,0:T(8,128)(2,1)}, u32[]{:S(2)}) %copy-start.4) | copy-done | bytes 1179672
  15.1 9.3 %own_rows.1 = (f32[512,1152]{1,0:T(8,128)S(1)}, bf16[512,1152]{1,0:T(8,128)(2,1)S(1)}, f32[512,1]{1,0:T(8,128)S(1)}, bf16[1152,512]{1,0:T(8,128)(2,1)S(1)}, f32[...) custom-call(f32[2]{0:T(128)S(1)} %pad_maximum_fusion.scal, ...), custom_call_target="tpu_custom_call" | custom-call | flops 6794772480 | bytes 22646792 | tf_op jit(solution)/shard_map/own_rows/pallas_call | solution.py:189
  24.4 8.4 %own_texts.1 = (f32[512,1152]{1,0:T(8,128)S(1)}, bf16[1024,1152]{1,0:T(8,128)(2,1)S(1)}, f32[512,1]{1,0:T(8,128)S(1)}, bf16[1152,512]{1,0:T(8,128)(2,1)S(1)}, f3...) custom-call(f32[2]{0:T(128)S(1)} %pad_maximum_fusion.scal, bf16[512,1152]{1,0:T(8,128)(2,1)} %collective-permute-done.image1, ...), custom_call_target="tpu_custom_call" | custom-call | flops 5435817984 | bytes 21172232 | tf_op jit(solution)/shard_map/own_texts/pallas_call | solution.py:189
  32.9 2.4 %collective-permute-done.1.text2 = bf16[512,1152]{1,0:T(8,128)(2,1)} collective-permute-done((bf16[512,1152]{1,0:T(8,128)(2,1)}, bf16[512,1152]{1,0:T(8,128)(2,1)}, u32[]{:S(2)}, u32[]{:S(2)}) %collective-permute-start.1) | collective-permute-done | bytes 1179680 | tf_op jit(solution)/shard_map/ppermute | solution.py:52
  35.3 10.6 %far_texts.1 = (bf16[1024,1152]{1,0:T(8,128)(2,1)S(1)}, bf16[512,1152]{1,0:T(8,128)(2,1)S(1)}, bf16[1152,512]{1,0:T(8,128)(2,1)S(1)}) custom-call(f32[2]{0:T(128)S(1)} %pad_maximum_fusion.scal, bf16[512,1152]{1,0:T(8,128)(2,1)} %collective-permute-done.1.text2, bf16[1152,1152]{1,0:T(8,128)(2,1)S(1)} %copy-done.2, bf16[1152,1152]{1,0:T(8,128)(2,1)S(1)} %fusion.shuffle, ...), custom_call_target="tpu_custom_call" | custom-call | flops 6794772480 | bytes 23007240 | tf_op jit(solution)/shard_map/far_texts/pallas_call | solution.py:189
  45.9 3.4 %away.1 = bf16[1152,1152]{1,0:T(8,128)(2,1)S(1)} custom-call(s32[1]{0:T(128)} %bitcast.which, bf16[1152,512]{1,0:T(8,128)(2,1)S(1)} %get-tuple-element.25.turn_i0, bf16[1152,512]{1,0:T(8,128)(2,1)S(1)} %get-tuple-element.31.turn_i1, bf16[1024,1152]{1,0:T(8,128)(2,1)S(1)} %get-tuple-element.39.delta_i, bf16[1152,512]{1,0:T(8,128)(2,1)S(1)} %get-tuple-element.40.turn_t0, ...), custom_call_target="tpu_custom_call" | custom-call | flops 2717908992 | bytes 12091396 | tf_op jit(solution)/shard_map/away/pallas_call | solution.py:189
  49.3 7.8 %collective-permute-start.2 = (bf16[1152,1152]{1,0:T(8,128)(2,1)S(1)}, bf16[1152,1152]{1,0:T(8,128)(2,1)S(1)}, u32[]{:S(2)}, u32[]{:S(2)}) collective-permute-start(bf16[1152,1152]{1,0:T(8,128)(2,1)S(1)} %away.1), channel_id=1, source_target_pairs={{0,1},{1,0},{2,3},{3,2},{4,5},{5,4},{6,7},{7,6},{8,9},{9,8},{10,11... | collective-permute-start | bytes 7962632 | tf_op jit(solution)/shard_map/ppermute | solution.py:251
  57.1 3.4 %kept.1 = f32[1152,1152]{1,0:T(8,128)S(1)} custom-call(s32[1]{0:T(128)} %bitcast.which, bf16[1152,512]{1,0:T(8,128)(2,1)S(1)} %get-tuple-element.25.turn_i0, bf16[1152,512]{1,0:T(8,128)(2,1)S(1)} %get-tuple-element.31.turn_i1, bf16[1024,1152]{1,0:T(8,128)(2,1)S(1)} %get-tuple-element.39.delta_i, bf16[1152,512]{1,0:T(8,128)(2,1)S(1)} %get-tuple-element.40.turn_t0, ...), custom_call_target="tpu_custom_call" | custom-call | flops 2717908992 | bytes 14745604 | tf_op jit(solution)/shard_map/kept/pallas_call | solution.py:189
  60.6 1.2 collective-permute-done.2
  61.7 0.6 add_convert_fusion
  62.3 36.6 %all_to_all.10.plane = bf16[16,72,1152]{2,1,0:T(8,128)(2,1)S(1)} all-to-all(bf16[16,72,1152]{2,1,0:T(8,128)(2,1)S(1)} %bitcast.10), channel_id=1, replica_groups={{0,2,4,6,64,66,68,70,128,130,132,134,192,194,196,198},{1,3,5,7,65,67,69..., dimensions={0} | all-to-all | bytes 5308416 | tf_op jit(solution)/shard_map/all_to_all | solution.py:256
  98.9 1.3 %join.1 = bf16[16,8,768]{2,1,0:T(8,128)(2,1)} custom-call(bf16[16,72,1152]{2,1,0:T(8,128)(2,1)S(1)} %all_to_all.10.plane), custom_call_target="tpu_custom_call" | custom-call | bytes 2850816 | tf_op jit(solution)/shard_map/join/pallas_call | solution.py:189
  100.2 7.3 %all-to-all-start.1 = ((bf16[16,8,768]{2,1,0:T(8,128)(2,1)}), bf16[16,8,768]{2,1,0:T(8,128)(2,1)S(1)}, u32[]{:S(2)}, u32[]{:S(2)}) async-start(bf16[16,8,768]{2,1,0:T(8,128)(2,1)} %join.1), calls=%async_computation.1 | async-start | bytes 393216 | tf_op jit(solution)/shard_map/all_to_all | solution.py:260
  107.5 10.3 %all-to-all-done.1 = bf16[16,8,768]{2,1,0:T(8,128)(2,1)S(1)} async-done(((bf16[16,8,768]{2,1,0:T(8,128)(2,1)}), bf16[16,8,768]{2,1,0:T(8,128)(2,1)S(1)}, u32[]{:S(2)}, u32[]{:S(2)}) %all-to-all-start.1) | async-done | bytes 196640 | tf_op jit(solution)/shard_map/all_to_all | solution.py:260
  118.0 0.2 fusion.2
  118.2 0.7 slice_reduce_fusion
  (17 shorter events, 0.1 us)
Async XLA Ops:
  3.8 20.6 %collective-permute-start = (bf16[512,1152]{1,0:T(8,128)(2,1)}, bf16[512,1152]{1,0:T(8,128)(2,1)}, u32[]{:S(2)}, u32[]{:S(2)}) collective-permute-start(bf16[512,1152]{1,0:T(8,128)(2,1)} %get-tuple-element.24.image), channel_id=1, source_target_pairs={{0,255},{1,0},{2,1},{3,2},{4,3},{5,4},{6,5},{7,6},{8,7},{9,8},{10,... | collective-permute-start | bytes 3538952 | tf_op jit(solution)/shard_map/ppermute | solution.py:52
  7.1 28.2 %collective-permute-start.1 = (bf16[512,1152]{1,0:T(8,128)(2,1)}, bf16[512,1152]{1,0:T(8,128)(2,1)}, u32[]{:S(2)}, u32[]{:S(2)}) collective-permute-start(bf16[512,1152]{1,0:T(8,128)(2,1)} %get-tuple-element.23.text), channel_id=1, source_target_pairs={{0,2},{1,3},{2,4},{3,5},{4,6},{5,7},{6,8},{7,9},{8,10},{9,11},{10,... | collective-permute-start | bytes 3538952 | tf_op jit(solution)/shard_map/ppermute | solution.py:52
  9.1 1.8 %copy-start = (bf16[1152,1152]{1,0:T(8,128)(2,1)S(1)}, bf16[1152,1152]{1,0:T(8,128)(2,1)}, u32[]{:S(2)}) copy-start(bf16[1152,1152]{1,0:T(8,128)(2,1)} %image_proj.3) | copy-start | bytes 7962628
  10.8 1.7 %copy-start.2 = (bf16[1152,1152]{1,0:T(8,128)(2,1)S(1)}, bf16[1152,1152]{1,0:T(8,128)(2,1)}, u32[]{:S(2)}) copy-start(bf16[1152,1152]{1,0:T(8,128)(2,1)} %text_proj.3) | copy-start | bytes 7962628
  12.6 1.3 %copy-start.3 = (bf16[512,1152]{1,0:T(8,128)(2,1)S(1)}, bf16[512,1152]{1,0:T(8,128)(2,1)}, u32[]{:S(2)}) copy-start(bf16[512,1152]{1,0:T(8,128)(2,1)} %get-tuple-element.23.text) | copy-start | bytes 3538948
  13.9 1.3 %copy-start.4 = (bf16[512,1152]{1,0:T(8,128)(2,1)S(1)}, bf16[512,1152]{1,0:T(8,128)(2,1)}, u32[]{:S(2)}) copy-start(bf16[512,1152]{1,0:T(8,128)(2,1)} %get-tuple-element.24.image) | copy-start | bytes 3538948
  15.1 9.3 %copy-start.1 = (bf16[1152,1152]{1,0:T(8,128)(2,1)S(1)}, bf16[1152,1152]{1,0:T(8,128)(2,1)}, u32[]{:S(2)}) copy-start(bf16[1152,1152]{1,0:T(8,128)(2,1)} %image_proj.3) | copy-start | bytes 7962628
  49.3 12.4 %collective-permute-start.2 = (bf16[1152,1152]{1,0:T(8,128)(2,1)S(1)}, bf16[1152,1152]{1,0:T(8,128)(2,1)S(1)}, u32[]{:S(2)}, u32[]{:S(2)}) collective-permute-start(bf16[1152,1152]{1,0:T(8,128)(2,1)S(1)} %away.1), channel_id=1, source_target_pairs={{0,1},{1,0},{2,3},{3,2},{4,5},{5,4},{6,7},{7,6},{8,9},{9,8},{10,11... | collective-permute-start | bytes 7962632 | tf_op jit(solution)/shard_map/ppermute | solution.py:251
  100.2 17.6 %all-to-all-start.1 = ((bf16[16,8,768]{2,1,0:T(8,128)(2,1)}), bf16[16,8,768]{2,1,0:T(8,128)(2,1)S(1)}, u32[]{:S(2)}, u32[]{:S(2)}) async-start(bf16[16,8,768]{2,1,0:T(8,128)(2,1)} %join.1), calls=%async_computation.1 | async-start | bytes 393216 | tf_op jit(solution)/shard_map/all_to_all | solution.py:260

commit v3 on v2

--- a/solution.py
+++ b/solution.py
@@ -210,8 +210,9 @@
         name="live_rows",
     )(counts, text_feat, image_feat)
     text2 = shift(text0, 2)
+    shuffle = shuffle_matrix()
+    image0, shuffle = lax.optimization_barrier((image0, shuffle))
     image1 = shift(image0, -1)
-    shuffle = shuffle_matrix()
     me = lax.axis_index("dp")
     core = me % 2
 

time: 119 us -> 119 us (level)
  transfers between devices with their start and end apart: 4 -> 4, of which waited for: 3 -> 3; matrix products, arithmetic and copies ran while one was open for 1% -> 0% of each run, Pallas kernels for 18% -> 18%
where the time goes in v3:
time: 119 us
  Pallas kernels  39 us (33%)
  blocking collectives  36.6 us (31%)
  starting transfers between devices  17.7 us (15%)
  waiting for transfers between devices  14.4 us (12%)
  local copies, waits for them, and re-layouts  6.81 us (6%)
  between operations  2.76 us (2%)
  other arithmetic  1.44 us (1%)
    all_to_all x1, blocking collectives, local(): lax.all_to_all(chip, 'dp', 0, 0, axis_index_groups=PLANES, tiled=True)  36.6 us
    pallas_call x6, Pallas kernels, call(): pl.pallas_call(kernel, out_shape=shapes, in_specs=[SMEM if a.size < 8 els...  36.4 us
    all_to_all x1, waiting for transfers between devices, local(): lax.all_to_all(plane, 'dp', 0, 0, axis_index_groups=COLUMNS, tiled=True)  10.3 us
    ppermute x1, starting transfers between devices, local(): back = lax.ppermute(away, 'dp', SWAP)  7.63 us
    all_to_all x1, starting transfers between devices, local(): lax.all_to_all(plane, 'dp', 0, 0, axis_index_groups=COLUMNS, tiled=True)  6.79 us
    unnamed x13, local copies, waits for them, and re-layouts  6.07 us
    ppermute x2, starting transfers between devices, shift(): return lax.ppermute(value, 'dp', [(d, (d + steps) % N) for d in range(N)])  3.32 us
    ppermute x2, waiting for transfers between devices, shift(): return lax.ppermute(value, 'dp', [(d, (d + steps) % N) for d in range(N)])  2.92 us
  transfers between devices with their start and end apart: 4, of which 3 were waited for; matrix products, arithmetic and copies ran while one was open for 0% of the time, Pallas kernels for 18%

profile of v3, /device:TPU:1, one launch (start us, length us, event | category | flops | bytes accessed | tf_op | source)
XLA Modules:
  0.0 118.7 jit_solution(8273271755300981689)
XLA Ops:
  1.3 0.5 fusion.shuffle
  1.8 2.5 %live_rows.1 = (bf16[512,1152]{1,0:T(8,128)(2,1)}, bf16[512,1152]{1,0:T(8,128)(2,1)}) custom-call(s32[1]{0:T(128)S(6)} %copy.13.count, bf16[512,1152]{1,0:T(8,128)(2,1)} %text.1, bf16[512,1152]{1,0:T(8,128)(2,1)} %image.1), custom_call_target="tpu_custom_call" | custom-call | tf_op jit(solution)/shard_map/live_rows/pallas_call | solution.py:203
  4.4 3.3 %collective-permute-start = (bf16[512,1152]{1,0:T(8,128)(2,1)}, bf16[512,1152]{1,0:T(8,128)(2,1)}, u32[]{:S(2)}, u32[]{:S(2)}) collective-permute-start(bf16[512,1152]{1,0:T(8,128)(2,1)} %get-tuple-element.27.image), channel_id=1, source_target_pairs={{0,255},{1,0},{2,1},{3,2},{4,3},{5,4},{6,5},{7,6},{8,7},{9,8},{10,... | collective-permute-start | bytes 3538952 | tf_op jit(solution)/shard_map/ppermute | solution.py:52
  7.7 0.0 collective-permute-start.1
  9.0 0.1 pad_maximum_fusion.scal
  9.1 1.7 %copy-done = bf16[1152,1152]{1,0:T(8,128)(2,1)S(1)} copy-done((bf16[1152,1152]{1,0:T(8,128)(2,1)S(1)}, bf16[1152,1152]{1,0:T(8,128)(2,1)}, u32[]{:S(2)}) %copy-start) | copy-done | bytes 2654232
  10.9 1.7 %copy-done.2 = bf16[1152,1152]{1,0:T(8,128)(2,1)S(1)} copy-done((bf16[1152,1152]{1,0:T(8,128)(2,1)S(1)}, bf16[1152,1152]{1,0:T(8,128)(2,1)}, u32[]{:S(2)}) %copy-start.2) | copy-done | bytes 2654232
  12.6 1.3 %copy-done.3 = bf16[512,1152]{1,0:T(8,128)(2,1)S(1)} copy-done((bf16[512,1152]{1,0:T(8,128)(2,1)S(1)}, bf16[512,1152]{1,0:T(8,128)(2,1)}, u32[]{:S(2)}) %copy-start.3) | copy-done | bytes 1179672
  13.9 1.3 %copy-done.4 = bf16[512,1152]{1,0:T(8,128)(2,1)S(1)} copy-done((bf16[512,1152]{1,0:T(8,128)(2,1)S(1)}, bf16[512,1152]{1,0:T(8,128)(2,1)}, u32[]{:S(2)}) %copy-start.4) | copy-done | bytes 1179672
  15.1 9.3 %own_rows.1 = (f32[512,1152]{1,0:T(8,128)S(1)}, bf16[512,1152]{1,0:T(8,128)(2,1)S(1)}, f32[512,1]{1,0:T(8,128)S(1)}, bf16[1152,512]{1,0:T(8,128)(2,1)S(1)}, f32[...) custom-call(f32[2]{0:T(128)S(1)} %pad_maximum_fusion.scal, ...), custom_call_target="tpu_custom_call" | custom-call | flops 6794772480 | bytes 22646792 | tf_op jit(solution)/shard_map/own_rows/pallas_call | solution.py:189
  24.4 8.5 %own_texts.1 = (f32[512,1152]{1,0:T(8,128)S(1)}, bf16[1024,1152]{1,0:T(8,128)(2,1)S(1)}, f32[512,1]{1,0:T(8,128)S(1)}, bf16[1152,512]{1,0:T(8,128)(2,1)S(1)}, f3...) custom-call(f32[2]{0:T(128)S(1)} %pad_maximum_fusion.scal, bf16[512,1152]{1,0:T(8,128)(2,1)} %collective-permute-done.image1, ...), custom_call_target="tpu_custom_call" | custom-call | flops 5435817984 | bytes 21172232 | tf_op jit(solution)/shard_map/own_texts/pallas_call | solution.py:189
  32.9 2.9 %collective-permute-done.1.text2 = bf16[512,1152]{1,0:T(8,128)(2,1)} collective-permute-done((bf16[512,1152]{1,0:T(8,128)(2,1)}, bf16[512,1152]{1,0:T(8,128)(2,1)}, u32[]{:S(2)}, u32[]{:S(2)}) %collective-permute-start.1) | collective-permute-done | bytes 1179680 | tf_op jit(solution)/shard_map/ppermute | solution.py:52
  35.9 10.6 %far_texts.1 = (bf16[1024,1152]{1,0:T(8,128)(2,1)S(1)}, bf16[512,1152]{1,0:T(8,128)(2,1)S(1)}, bf16[1152,512]{1,0:T(8,128)(2,1)S(1)}) custom-call(f32[2]{0:T(128)S(1)} %pad_maximum_fusion.scal, bf16[512,1152]{1,0:T(8,128)(2,1)} %collective-permute-done.1.text2, bf16[1152,1152]{1,0:T(8,128)(2,1)S(1)} %copy-done.2, bf16[1152,1152]{1,0:T(8,128)(2,1)S(1)} %fusion.shuffle, ...), custom_call_target="tpu_custom_call" | custom-call | flops 6794772480 | bytes 23007240 | tf_op jit(solution)/shard_map/far_texts/pallas_call | solution.py:189
  46.4 3.4 %away.1 = bf16[1152,1152]{1,0:T(8,128)(2,1)S(1)} custom-call(s32[1]{0:T(128)} %bitcast.which, bf16[1152,512]{1,0:T(8,128)(2,1)S(1)} %get-tuple-element.29.turn_i0, bf16[1152,512]{1,0:T(8,128)(2,1)S(1)} %get-tuple-element.35.turn_i1, bf16[1024,1152]{1,0:T(8,128)(2,1)S(1)} %get-tuple-element.43.delta_i, bf16[1152,512]{1,0:T(8,128)(2,1)S(1)} %get-tuple-element.44.turn_t0, ...), custom_call_target="tpu_custom_call" | custom-call | flops 2717908992 | bytes 12091396 | tf_op jit(solution)/shard_map/away/pallas_call | solution.py:189
  49.9 7.6 %collective-permute-start.2 = (bf16[1152,1152]{1,0:T(8,128)(2,1)S(1)}, bf16[1152,1152]{1,0:T(8,128)(2,1)S(1)}, u32[]{:S(2)}, u32[]{:S(2)}) collective-permute-start(bf16[1152,1152]{1,0:T(8,128)(2,1)S(1)} %away.1), channel_id=1, source_target_pairs={{0,1},{1,0},{2,3},{3,2},{4,5},{5,4},{6,7},{7,6},{8,9},{9,8},{10,11... | collective-permute-start | bytes 7962632 | tf_op jit(solution)/shard_map/ppermute | solution.py:252
  57.5 3.4 %kept.1 = f32[1152,1152]{1,0:T(8,128)S(1)} custom-call(s32[1]{0:T(128)} %bitcast.which, bf16[1152,512]{1,0:T(8,128)(2,1)S(1)} %get-tuple-element.29.turn_i0, bf16[1152,512]{1,0:T(8,128)(2,1)S(1)} %get-tuple-element.35.turn_i1, bf16[1024,1152]{1,0:T(8,128)(2,1)S(1)} %get-tuple-element.43.delta_i, bf16[1152,512]{1,0:T(8,128)(2,1)S(1)} %get-tuple-element.44.turn_t0, ...), custom_call_target="tpu_custom_call" | custom-call | flops 2717908992 | bytes 14745604 | tf_op jit(solution)/shard_map/kept/pallas_call | solution.py:189
  60.9 1.2 collective-permute-done.2
  62.1 0.6 add_convert_fusion
  62.7 36.6 %all_to_all.10.plane = bf16[16,72,1152]{2,1,0:T(8,128)(2,1)S(1)} all-to-all(bf16[16,72,1152]{2,1,0:T(8,128)(2,1)S(1)} %bitcast.10), channel_id=1, replica_groups={{0,2,4,6,64,66,68,70,128,130,132,134,192,194,196,198},{1,3,5,7,65,67,69..., dimensions={0} | all-to-all | bytes 5308416 | tf_op jit(solution)/shard_map/all_to_all | solution.py:257
  99.3 1.3 %join.1 = bf16[16,8,768]{2,1,0:T(8,128)(2,1)} custom-call(bf16[16,72,1152]{2,1,0:T(8,128)(2,1)S(1)} %all_to_all.10.plane), custom_call_target="tpu_custom_call" | custom-call | bytes 2850816 | tf_op jit(solution)/shard_map/join/pallas_call | solution.py:189
  100.6 6.8 %all-to-all-start.1 = ((bf16[16,8,768]{2,1,0:T(8,128)(2,1)}), bf16[16,8,768]{2,1,0:T(8,128)(2,1)S(1)}, u32[]{:S(2)}, u32[]{:S(2)}) async-start(bf16[16,8,768]{2,1,0:T(8,128)(2,1)} %join.1), calls=%async_computation.1 | async-start | bytes 393216 | tf_op jit(solution)/shard_map/all_to_all | solution.py:261
  107.3 10.3 %all-to-all-done.1 = bf16[16,8,768]{2,1,0:T(8,128)(2,1)S(1)} async-done(((bf16[16,8,768]{2,1,0:T(8,128)(2,1)}), bf16[16,8,768]{2,1,0:T(8,128)(2,1)S(1)}, u32[]{:S(2)}, u32[]{:S(2)}) %all-to-all-start.1) | async-done | bytes 196640 | tf_op jit(solution)/shard_map/all_to_all | solution.py:261
  117.8 0.2 fusion.2
  118.0 0.7 slice_reduce_fusion
  (17 shorter events, 0.1 us)
Async XLA Ops:
  4.4 20.1 %collective-permute-start = (bf16[512,1152]{1,0:T(8,128)(2,1)}, bf16[512,1152]{1,0:T(8,128)(2,1)}, u32[]{:S(2)}, u32[]{:S(2)}) collective-permute-start(bf16[512,1152]{1,0:T(8,128)(2,1)} %get-tuple-element.27.image), channel_id=1, source_target_pairs={{0,255},{1,0},{2,1},{3,2},{4,3},{5,4},{6,5},{7,6},{8,7},{9,8},{10,... | collective-permute-start | bytes 3538952 | tf_op jit(solution)/shard_map/ppermute | solution.py:52
  7.7 28.2 %collective-permute-start.1 = (bf16[512,1152]{1,0:T(8,128)(2,1)}, bf16[512,1152]{1,0:T(8,128)(2,1)}, u32[]{:S(2)}, u32[]{:S(2)}) collective-permute-start(bf16[512,1152]{1,0:T(8,128)(2,1)} %get-tuple-element.25.text), channel_id=1, source_target_pairs={{0,2},{1,3},{2,4},{3,5},{4,6},{5,7},{6,8},{7,9},{8,10},{9,11},{10,... | collective-permute-start | bytes 3538952 | tf_op jit(solution)/shard_map/ppermute | solution.py:52
  9.1 1.8 %copy-start = (bf16[1152,1152]{1,0:T(8,128)(2,1)S(1)}, bf16[1152,1152]{1,0:T(8,128)(2,1)}, u32[]{:S(2)}) copy-start(bf16[1152,1152]{1,0:T(8,128)(2,1)} %image_proj.3) | copy-start | bytes 7962628
  10.8 1.7 %copy-start.2 = (bf16[1152,1152]{1,0:T(8,128)(2,1)S(1)}, bf16[1152,1152]{1,0:T(8,128)(2,1)}, u32[]{:S(2)}) copy-start(bf16[1152,1152]{1,0:T(8,128)(2,1)} %text_proj.3) | copy-start | bytes 7962628
  12.6 1.3 %copy-start.3 = (bf16[512,1152]{1,0:T(8,128)(2,1)S(1)}, bf16[512,1152]{1,0:T(8,128)(2,1)}, u32[]{:S(2)}) copy-start(bf16[512,1152]{1,0:T(8,128)(2,1)} %get-tuple-element.25.text) | copy-start | bytes 3538948
  13.9 1.3 %copy-start.4 = (bf16[512,1152]{1,0:T(8,128)(2,1)S(1)}, bf16[512,1152]{1,0:T(8,128)(2,1)}, u32[]{:S(2)}) copy-start(bf16[512,1152]{1,0:T(8,128)(2,1)} %get-tuple-element.27.image) | copy-start | bytes 3538948
  15.1 9.3 %copy-start.1 = (bf16[1152,1152]{1,0:T(8,128)(2,1)S(1)}, bf16[1152,1152]{1,0:T(8,128)(2,1)}, u32[]{:S(2)}) copy-start(bf16[1152,1152]{1,0:T(8,128)(2,1)} %image_proj.3) | copy-start | bytes 7962628
  49.9 12.2 %collective-permute-start.2 = (bf16[1152,1152]{1,0:T(8,128)(2,1)S(1)}, bf16[1152,1152]{1,0:T(8,128)(2,1)S(1)}, u32[]{:S(2)}, u32[]{:S(2)}) collective-permute-start(bf16[1152,1152]{1,0:T(8,128)(2,1)S(1)} %away.1), channel_id=1, source_target_pairs={{0,1},{1,0},{2,3},{3,2},{4,5},{5,4},{6,7},{7,6},{8,9},{9,8},{10,11... | collective-permute-start | bytes 7962632 | tf_op jit(solution)/shard_map/ppermute | solution.py:252
  100.6 17.1 %all-to-all-start.1 = ((bf16[16,8,768]{2,1,0:T(8,128)(2,1)}), bf16[16,8,768]{2,1,0:T(8,128)(2,1)S(1)}, u32[]{:S(2)}, u32[]{:S(2)}) async-start(bf16[16,8,768]{2,1,0:T(8,128)(2,1)} %join.1), calls=%async_computation.1 | async-start | bytes 393216 | tf_op jit(solution)/shard_map/all_to_all | solution.py:261
